TPU v7x, 32 devices: a whole 2x2x4 slice. The times are simulated.
32 devices in a mesh: scen: 2 (over x), row: 16 (over z, y, core).
Axes of the slice: x: 2, y: 2, z: 4, core: 2. Of those that a mesh axis runs over, the one named last changes fastest.
Arguments:
- basin_state: float32 [6, 256, 2048], P('scen', 'row'), parts along dimension 0, may hold values from -1.5 to 1.5
- basin_depth: float32 [256, 4096], P('row', 'scen'), parts along dimension 1, may hold values from 0.7 to 1.5
- coast_depth: float32 [16, 512, 256], P('row', 'scen'), parts along dimension 1, may hold values from 0.1 to 2
- coast_flow: float32 [16, 4, 256, 256], P('row', 'scen'), parts along dimension 1, may hold values from -0.4 to 0.4
- coast_link: int32 [16, 6], P('row', 'scen'), parts along dimension 1, may hold values from 0 to 2031, as said below
Outputs:
- basin_out: float32 [6, 256, 2048], P('scen', 'row'), parts along dimension 0
- coast_out: float32 [16, 6, 256, 256], P('row', 'scen'), parts along dimension 1
There are 2 independent parts, one for each index of `scen`. A program takes and returns all parts, laid end to end along the dimension named above; each array names one. Nothing has to cross between parts.
Inputs may be any that keep to these rules, and one draw needn't show every extreme that they name: `coast_link`: column 0 is a basin row below 256, column 1 a column at most 2031, column 2 is 0 or 1; block 0 links to the last row and last start column, block 1 to row 0 and column 0.
All inputs are finite; a program needn't handle non-finite values.
Results may differ from a plain program's by a relative error of at most 0.0003.
Values sent between devices are 32-bit elements; how exact they have to be, the bound alone decides.
No kernel may reach another device: no remote copies, remote signals or barrier semaphores. Data moves between devices by JAX's collectives and lax.ppermute only.
A program may use at most 64 MiB of HBM per device.

v0:
```python
import functools

import jax
import jax.numpy as jnp
from jax import lax
from jax.experimental import pallas as pl
from jax.experimental.pallas import tpu as pltpu
from jax.sharding import PartitionSpec as P

BSTEPS = 8
CSTEPS = 10

depth_floor = 0.2
ghost_level = 2.0

RATE = 0.05
DEPTH_UNIT = RATE * RATE
FLOW_UNIT = RATE * RATE * RATE
TINY = 1e-30

HALO = BSTEPS
SUB = 8
LANES = 128


def lane_ids():
    return lax.broadcasted_iota(jnp.int32, (SUB, LANES), 1)


def row_ids():
    return lax.broadcasted_iota(jnp.int32, (SUB, LANES), 0)


def cell_terms(u):
    h, mu, mv = u
    r = pl.reciprocal(jnp.maximum(h, depth_floor * DEPTH_UNIT), approx=True)
    vx, vy = mu * r, mv * r
    hp = jnp.maximum(h, TINY)
    c = hp * lax.rsqrt(hp)
    p = (0.5 * h) * h
    cross = mu * vy
    return {
        "u": u,
        "fx": (mu, mu * vx + p, cross),
        "fy": (mv, cross, mv * vy + p),
        "sx": jnp.abs(vx) + c,
        "sy": jnp.abs(vy) + c,
    }


def y_face(above, below):
    a = jnp.maximum(above["sy"], below["sy"])
    return [
        a * (ub - ua) - (fa + fb)
        for ua, ub, fa, fb in zip(above["u"], below["u"], above["fy"], below["fy"])
    ]


def coast_steps(state, terms, after, parts, opening, rows, group, steps, ghost):
    lane, sub = lane_ids(), row_ids()
    first, last = lane == 0, lane == LANES - 1
    top, bottom = sub == 0, sub == SUB - 1
    zero = jnp.zeros((SUB, LANES), jnp.float32)
    left = functools.partial(pltpu.roll, shift=LANES - 1, axis=1)
    right = functools.partial(pltpu.roll, shift=1, axis=1)

    def load(view, k):
        return [[view[f, half, 1 + k] for f in range(3)] for half in range(2)]

    def store(view, k, both):
        for half in range(2):
            for f in range(3):
                view[f, half, 1 + k] = both[half][f]

    def store_above(tails):
        store(state, -1, [[jnp.where(top, g, pltpu.roll(t, 1, 0)) for g, t in zip(*pair)] for pair in zip(ghost, tails)])

    def y_terms_of(view, k):
        both = [cell_terms(u) for u in load(view, k)]
        for half, cell in enumerate(both):
            terms[half, 1 + k, 0] = cell["sy"]
            terms[half, 1 + k, 1] = cell["fy"][2]
            terms[half, 1 + k, 2] = cell["fx"][2]
        return both

    def terms_of(view, k):
        even, odd = y_terms_of(view, k)
        for half, cell in enumerate((even, odd)):
            terms[half, 1 + k, 3] = cell["sx"]
            terms[half, 1 + k, 4] = cell["fx"][1]
        moved = zip(even["u"] + [even["sx"]] + list(even["fx"][1:]), odd["u"] + [odd["sx"]] + list(odd["fx"][1:]))
        for q, (e, o) in enumerate(moved):
            after[k, q] = jnp.where(last, o, left(e))

    def x_faces(view, k):
        even, odd = load(view, k)
        following = [after[k, f] for f in range(3)]
        sx_e, sx_o, sx_n = terms[0, 1 + k, 3], terms[1, 1 + k, 3], after[k, 3]
        fx_e = [even[1], terms[0, 1 + k, 4], terms[0, 1 + k, 2]]
        fx_o = [odd[1], terms[1, 1 + k, 4], terms[1, 1 + k, 2]]
        fx_n = [following[1], after[k, 4], after[k, 5]]
        a_in, a_out = jnp.maximum(sx_e, sx_o), jnp.maximum(sx_o, sx_n)
        for f in range(3):
            g_in = a_in * (odd[f] - even[f]) - (fx_e[f] + fx_o[f])
            g_out = a_out * (following[f] - odd[f]) - (fx_o[f] + fx_n[f])
            g_back = jnp.where(first, -2.0 * fx_e[f], right(g_out))
            parts[k, f] = even[f] + (g_in - g_back)
            parts[k, 3 + f] = odd[f] + (g_out - g_in)

    def y_cells(view, k):
        return [
            {
                "u": u,
                "fy": [u[2], terms[half, 1 + k, 2], terms[half, 1 + k, 1]],
                "sy": terms[half, 1 + k, 0],
            }
            for half, u in enumerate(load(view, k))
        ]

    def trip(i, acc):
        view = state.at[:, :, pl.ds(i * group, 1 + group)]
        y_terms_of(view, -1)
        for k in range(group):
            terms_of(view, k)
        for k in range(group):
            x_faces(view, k)
        prev = y_cells(view, -1)
        for k in range(group):
            cur = y_cells(view, k)
            face = [y_face(a, b) for a, b in zip(prev, cur)]
            if k == 0:
                for half in range(2):
                    for f in range(3):
                        opening[i, half, f] = pltpu.roll(face[half][f], SUB - 1, 0)
            store(view, k - 1, [[x + g for x, g in zip(*pair)] for pair in zip(acc, face)])
            acc = [[parts[k, 3 * half + f] - face[half][f] for f in range(3)] for half in range(2)]
            prev = cur
        return acc

    def step(_, carry):
        acc = lax.fori_loop(0, rows // group, trip, [[zero] * 3 for _ in range(2)])
        tails = [
            [
                x + jnp.where(bottom, -2.0 * f, opening[0, half, i])
                for i, (x, f) in enumerate(zip(xs, cell["fy"]))
            ]
            for half, (xs, cell) in enumerate(
                zip(acc, y_cells(state.at[:, :, rows - group :], group - 1))
            )
        ]
        store(state, rows - 1, tails)
        store_above(tails)
        return carry

    store_above(load(state, rows - 1))
    lax.fori_loop(0, steps, step, 0)


GROUP = 16
UNITS = (DEPTH_UNIT, FLOW_UNIT, FLOW_UNIT)
VMEM_LIMIT = 12 * 1024 * 1024
HALF = LANES // 2


def pick(values, ids):
    return jnp.take_along_axis(values, ids, axis=1, mode="promise_in_bounds")


def split_columns(west, east):
    lane = lane_ids()
    low = lane < HALF
    twice = 2 * jnp.where(low, lane, lane - HALF)
    w = pick(west, jnp.where(low, twice, twice + 1))
    e = pick(east, jnp.where(low, twice + 1, twice))
    return jnp.where(low, w, e), pltpu.roll(jnp.where(low, e, w), HALF, 1)


def join_columns(even, odd):
    lane = lane_ids()
    low = lane < HALF
    odd = pltpu.roll(odd, HALF, 1)
    w, e = jnp.where(low, even, odd), jnp.where(low, odd, even)
    half, is_odd = lane // 2, lane % 2
    return pick(w, half + HALF * is_odd), pick(e, half + HALF * (1 - is_odd))


HALVES = (slice(0, LANES), slice(LANES, 2 * LANES))
TALL = 32


def fold_kernel(link, depth, flow, state, wet, tmp):
    rows = depth.shape[0] // SUB
    wet[...] = jnp.broadcast_to(link[:, 2:3], wet.shape).astype(jnp.float32)

    def copy_in(i, carry):
        at = pl.ds(pl.multiple_of(i * TALL, TALL), TALL)
        for f in range(3):
            raw = depth[at] if f == 0 else flow[f - 1, at]
            for p in range(2):
                tmp[f, p, at] = raw[:, HALVES[p]] * UNITS[f]
        return carry

    def fold_field(f, carry):
        def fold(k, carry):
            both = split_columns(*[tmp[f, p, pl.ds(k, SUB, stride=rows), :] for p in range(2)])
            for p in range(2):
                state[f, p, k] = both[p]
            return carry

        return lax.fori_loop(0, rows, fold, carry, unroll=rows)

    lax.fori_loop(0, depth.shape[0] // TALL, copy_in, 0)
    lax.fori_loop(0, 3, fold_field, 0)


def coast_fold(link, depth, flow):
    cells = depth.shape[0]
    vmem = pl.BlockSpec(memory_space=pltpu.VMEM)
    return pl.pallas_call(
        fold_kernel,
        out_shape=(
            jax.ShapeDtypeStruct((3, 2, cells // SUB, SUB, LANES), jnp.float32),
            jax.ShapeDtypeStruct((SUB, LANES), jnp.float32),
        ),
        in_specs=[vmem, vmem, vmem],
        out_specs=(vmem, vmem),
        scratch_shapes=[pltpu.VMEM((3, 2, cells, LANES), jnp.float32)],
        compiler_params=pltpu.CompilerParams(vmem_limit_bytes=VMEM_LIMIT),
        cost_estimate=pl.CostEstimate(
            flops=CSTEPS * 70 * cells * cells, bytes_accessed=24 * cells * cells, transcendentals=0
        ),
        name="coast_fold",
    )(link, depth, flow)


def coast_kernel(
    wet, ghosts, folded, depth, flow, out, state, terms, after, parts, opening, tmp, done, sems
):
    rows = depth.shape[0] // SUB
    is_wet = jnp.max(wet[...]) > 0.0

    def copy_in(k, carry):
        for f in range(3):
            for p in range(2):
                state[f, p, 1 + k] = folded[f, p, k]
        return carry

    @pl.when(jnp.logical_not(is_wet))
    def _():
        copies = [
            pltpu.make_async_copy(depth, out.at[0], sems.at[0]),
            pltpu.make_async_copy(flow, out.at[1:], sems.at[1]),
        ]
        for copy in copies:
            copy.start()
        for copy in copies:
            copy.wait()

    @pl.when(is_wet)
    def _():
        lax.fori_loop(0, rows, copy_in, 0, unroll=4)
        values = jnp.sum(ghosts[...], axis=0)
        level = (ghost_level + values) * DEPTH_UNIT
        inflow = values * FLOW_UNIT
        h, mv = [
            [jnp.broadcast_to(v[i : i + 1], (SUB, LANES)) for i in range(at, at + 2)]
            for v, at in ((level, 0), (inflow, 2))
        ]
        ghost = [[h[p], jnp.zeros_like(h[p]), mv[p]] for p in range(2)]
        coast_steps(state, terms, after, parts, opening, rows, GROUP, CSTEPS, ghost)

        def write(f):
            return pltpu.make_async_copy(done.at[f], out.at[f], sems.at[f])

        def finish(f, carry):
            scale = jnp.where(f == 0, 1.0 / DEPTH_UNIT, 1.0 / FLOW_UNIT)

            def unfold(k, carry):
                both = join_columns(state[f, 0, 1 + k], state[f, 1, 1 + k])
                for p in range(2):
                    tmp[p, pl.ds(k, SUB, stride=rows), :] = both[p] * scale
                return carry

            def copy_out(i, carry):
                at = pl.ds(pl.multiple_of(i * TALL, TALL), TALL)
                for p in range(2):
                    done[f, at, HALVES[p]] = tmp[p, at]
                return carry

            lax.fori_loop(0, rows, unfold, 0, unroll=rows)
            lax.fori_loop(0, depth.shape[0] // TALL, copy_out, 0, unroll=2)
            write(f).start()
            return carry

        lax.fori_loop(0, 3, finish, 0)
        for f in range(3):
            write(f).wait()


def coast_run(wet, ghosts, folded, depth, flow):
    cells = depth.shape[0]
    vmem = pl.BlockSpec(memory_space=pltpu.VMEM)
    return pl.pallas_call(
        coast_kernel,
        out_shape=jax.ShapeDtypeStruct((3, cells, cells), jnp.float32),
        in_specs=[vmem] * 5,
        out_specs=pl.BlockSpec(memory_space=pltpu.HBM),
        scratch_shapes=[
            pltpu.VMEM((3, 2, 1 + cells // SUB, SUB, LANES), jnp.float32),
            pltpu.VMEM((2, 1 + GROUP, 5, SUB, LANES), jnp.float32),
            pltpu.VMEM((GROUP, 6, SUB, LANES), jnp.float32),
            pltpu.VMEM((GROUP, 6, SUB, LANES), jnp.float32),
            pltpu.VMEM((cells // SUB // GROUP, 2, 3, SUB, LANES), jnp.float32),
            pltpu.VMEM((2, cells, LANES), jnp.float32),
            pltpu.VMEM((3, cells, cells), jnp.float32),
            pltpu.SemaphoreType.DMA((3,)),
        ],
        compiler_params=pltpu.CompilerParams(vmem_limit_bytes=VMEM_LIMIT),
        cost_estimate=pl.CostEstimate(
            flops=CSTEPS * 70 * cells * cells, bytes_accessed=24 * cells * cells, transcendentals=0
        ),
        name="coast_steps",
    )(wet, ghosts, folded, depth, flow)


def basin_kernel(state, depth, pair_state, pair_depth, edge, out, eta, hu, hv, dep):
    rows, width = depth.shape
    total = rows + 2 * HALO
    chunks = width // LANES
    position = lax.axis_index("row")
    odd = position % 2
    north_inside = (position < lax.axis_size("row") - 1).astype(jnp.float32)
    pair_from = pl.multiple_of(odd * (rows - HALO), HALO)
    pair_at = pl.multiple_of((1 - odd) * (HALO + rows), HALO)
    edge_at = pl.multiple_of(odd * (HALO + rows), HALO)
    for ref, field, unit in ((eta, 0, 1.0), (hu, 1, 0.5), (hv, 2, 0.5), (dep, 3, 0.25)):
        own, pair = (depth, pair_depth) if field == 3 else (state.at[field], pair_state.at[field])
        for c in range(chunks):
            at = slice(c * LANES, (c + 1) * LANES)
            ref[c, HALO : HALO + rows] = own[:, at] * unit
            ref[c, pl.ds(pair_at, HALO)] = pair[pl.ds(pair_from, HALO), at] * unit
            ref[c, pl.ds(edge_at, HALO)] = edge[field, :, at] * unit
    apart = total // SUB
    lane = lane_ids()
    first, last = lane == 0, lane == LANES - 1
    kept = jnp.where(row_ids() * apart < HALO + rows, 1.0, north_inside)
    zero = jnp.zeros((SUB, LANES), jnp.float32)

    def load(ref, c):
        return [ref[c, pl.ds(k, SUB, stride=apart), :] for k in range(apart)]

    def store(ref, c, values):
        for k in range(apart):
            ref[c, pl.ds(k, SUB, stride=apart), :] = values[k]

    def step(_, carry):
        prev_west = [zero] * apart
        prev_eta, prev_east, prev_hu = None, None, None
        for c in range(chunks + 1):
            if c < chunks:
                u, v, d = load(hu, c), load(hv, c), load(dep, c)
                west = [pltpu.roll(x, 1, 1) for x in u]
                south = [pltpu.roll(v[-1], 1, 0)] + v[:-1]
                new = [
                    (e - ((x - jnp.where(first, p, w)) + (y - t))) * kept
                    for e, x, p, w, y, t in zip(load(eta, c), u, prev_west, west, v, south)
                ]
                store(eta, c, new)
                east = [pltpu.roll(x, LANES - 1, 1) for x in new]
                north = new[1:] + [pltpu.roll(new[0], SUB - 1, 0)]
                store(hv, c, [y - g * (n - x) for y, g, n, x in zip(v, d, north, new)])
            else:
                east = [zero] * apart
            if c > 0:
                d = load(dep, c - 1)
                store(
                    hu,
                    c - 1,
                    [
                        x - g * (jnp.where(last, e, p) - n)
                        for x, g, e, p, n in zip(prev_hu, d, east, prev_east, prev_eta)
                    ],
                )
            prev_west, prev_eta, prev_east, prev_hu = west, new, east, u
        return carry

    lax.fori_loop(0, BSTEPS, step, 0)
    for c in range(chunks):
        at = slice(c * LANES, (c + 1) * LANES)
        for f, (ref, unit) in enumerate(((eta, 1.0), (hu, 2.0), (hv, 2.0))):
            out[f, :, at] = ref[c, HALO : HALO + rows] * unit


def basin_run(state, depth, pair_state, pair_depth, edge):
    rows, width = depth.shape
    total = rows + 2 * HALO
    vmem = pl.BlockSpec(memory_space=pltpu.VMEM)
    return pl.pallas_call(
        basin_kernel,
        out_shape=jax.ShapeDtypeStruct((3, rows, width), jnp.float32),
        in_specs=[vmem] * 5,
        out_specs=vmem,
        scratch_shapes=[pltpu.VMEM((width // LANES, total, LANES), jnp.float32)] * 4,
        compiler_params=pltpu.CompilerParams(vmem_limit_bytes=VMEM_LIMIT),
        cost_estimate=pl.CostEstimate(
            flops=BSTEPS * 16 * total * width, bytes_accessed=4 * 11 * rows * width, transcendentals=0
        ),
        name="basin_steps",
    )(state, depth, pair_state, pair_depth, edge)


def strips_kernel(links, own, pair, ghosts, strips):
    rows, width = own.shape[1], own.shape[2]
    count = ghosts.shape[0]
    span = 2 * LANES
    position = lax.axis_index("row")
    tops = (position * rows, (position + 1 - 2 * (position % 2)) * rows)
    lane = lane_ids()
    weight = ((2 * lane + row_ids() % 2) % 16).astype(jnp.float32) / 16.0 + 0.5 / 16.0

    def piece(b, carry):
        col = links[b, 0, 1]
        start = jnp.clip(col // LANES, 0, width // LANES - 2) * LANES
        shift = lax.rem(span - (col - start), span)
        at = pl.ds(pl.multiple_of(start, LANES), span)
        for i, f in enumerate((0, 2)):
            chunk = None
            for source, top in zip((own, pair), tops):
                row = links[b, 0, 0] - top
                owned = jnp.logical_and(row >= 0, row < rows).astype(jnp.float32)
                part = source[f, pl.ds(jnp.clip(row, 0, rows - 1), 1), at] * owned
                chunk = part if chunk is None else chunk + part
            moved = pltpu.roll(chunk, shift, 1)[:, :LANES]
            strips[b, 2 * i : 2 * i + 2] = jnp.broadcast_to(moved, (2, LANES))
        values = strips[b]
        low, high = pick(values, lane // 8), pick(values, lane // 8 + 1)
        ghosts[b] = (1.0 - weight) * low + weight * high
        return carry

    strips[...] = jnp.zeros_like(strips)
    lax.fori_loop(0, count, piece, 0, unroll=8)


def make_strips(links, own, pair):
    count = links.shape[0]
    tiles = (count, SUB, LANES)
    vmem = pl.BlockSpec(memory_space=pltpu.VMEM)
    smem = pl.BlockSpec(memory_space=pltpu.SMEM)
    return pl.pallas_call(
        strips_kernel,
        out_shape=jax.ShapeDtypeStruct(tiles, jnp.float32),
        in_specs=[smem, vmem, vmem],
        out_specs=vmem,
        scratch_shapes=[pltpu.VMEM(tiles, jnp.float32)],
        compiler_params=pltpu.CompilerParams(vmem_limit_bytes=VMEM_LIMIT),
        cost_estimate=pl.CostEstimate(flops=2 * 10**10, bytes_accessed=own.size, transcendentals=0),
        name="strips",
    )(links, own, pair)


def local(basin_state, basin_depth, coast_depth, coast_flow, coast_link):
    devices = lax.axis_size("row")
    odd = lax.axis_index("row") % 2
    chips = list(range(devices // 2))[::-1]
    chips.insert(0, chips.pop(len(chips) - 1 - devices // 4))
    parity = [[2 * chip + p for chip in chips] for p in range(2)]
    sent = jnp.broadcast_to(coast_link, (devices // 2,) + coast_link.shape)
    sent, later_state = lax.optimization_barrier((sent, basin_state))
    start = odd * (basin_depth.shape[0] - HALO)
    edge = jnp.concatenate(
        [
            lax.dynamic_slice_in_dim(later_state, start, HALO, axis=1),
            lax.dynamic_slice_in_dim(basin_depth, start, HALO, axis=0)[None],
        ],
        axis=0,
    )
    sent, edge = lax.optimization_barrier((sent, edge))
    links = lax.all_to_all(sent, "row", 0, 0, axis_index_groups=parity, tiled=True)

    twins = [(i, i ^ 1) for i in range(devices)]
    pair_state, pair_depth = [lax.ppermute(a, "row", twins) for a in (basin_state, basin_depth)]
    across = [(i, i + 1) for i in range(1, devices - 1, 2)]
    edge = lax.ppermute(edge, "row", across + [(j, i) for i, j in across])

    depth, flow = coast_depth[0], coast_flow[0]
    folded, wet = coast_fold(coast_link, depth, flow)
    pair_state, folded = lax.optimization_barrier((pair_state, folded))
    ghosts = make_strips(links, basin_state, pair_state)
    basin_depth, ghosts = lax.optimization_barrier((basin_depth, ghosts))
    ghosts = lax.all_to_all(ghosts, "row", 0, 0, axis_index_groups=parity, tiled=True)
    basin_out = basin_run(basin_state, basin_depth, pair_state, pair_depth, edge)
    folded, basin_out = lax.optimization_barrier((folded, basin_out))
    coast_out = coast_run(wet, ghosts, folded, depth, flow)
    return (basin_out, coast_out[None])


def solution(mesh):
    in_specs = (
        P("scen", "row", None),
        P("row", "scen"),
        P("row", "scen", None),
        P("row", "scen", None, None),
        P("row", "scen"),
    )
    out_specs = (P("scen", "row", None), P("row", "scen", None, None))
    return jax.shard_map(local, mesh=mesh, in_specs=in_specs, out_specs=out_specs, check_vma=False)
```

profile of v0, /device:TPU:0, one launch (start us, length us, event | category | flops | bytes accessed | tf_op | source)
XLA Modules:
  0.0 33.9 jit_solution(17977488988006652694)
XLA Ops:
  0.6 0.5 %collective-permute-start.1 = (f32[16,2048]{1,0:T(8,128)}, f32[16,2048]{1,0:T(8,128)S(1)}, u32[]{:S(2)}, u32[]{:S(2)}) collective-permute-start(f32[16,2048]{1,0:T(8,128)} %depth), channel_id=1, source_target_pairs={{0,1},{1,0},{2,3},{3,2},{4,5},{5,4},{6,7},{7,6},{8,9},{9,8},{10,11... | collective-permute-start | bytes 393224 | tf_op jit(solution)/shard_map/ppermute | solution.py:481
  1.1 0.1 collective-permute-start
  1.2 0.0 copy-start.4
  1.2 0.7 %copy-done.4 = s32[1,3]{1,0:T(1,128)S(1)} copy-done((s32[1,3]{1,0:T(1,128)S(1)}, s32[1,3]{1,0:T(1,128)}, u32[]{:S(2)}) %copy-start.4) | copy-done | bytes 36
  1.9 0.0 copy-start.3
  1.9 0.6 %broadcast_in_dim.9 = s32[8,1,3]{2,1,0:T(1,128)} broadcast(s32[3]{0:T(128)S(1)} %bitcast.10), dimensions={2} | broadcast | bytes 108 | tf_op jit(solution)/shard_map/broadcast_in_dim | solution.py:467
  2.5 0.0 copy-start
  2.5 1.0 %constant_dynamic-slice_fusion = f32[3,8,2048]{2,1,0:T(8,128)S(1)} fusion(f32[3,16,2048]{2,1,0:T(8,128)} %state.1, s32[]{:T(128)S(6)} %select_n.12), kind=kLoop, calls=%fused_computation.2 | loop fusion | bytes 393220 | tf_op jit(solution)/shard_map/dynamic_slice | solution.py:472
  3.5 0.0 copy-done.3
  3.5 0.0 copy-start.1
  3.6 8.0 %all-to-all-start = ((s32[8,1,3]{2,1,0:T(1,128)}), s32[8,1,3]{2,1,0:T(1,128)S(1)}, u32[]{:S(2)}, u32[]{:S(2)}) async-start(s32[8,1,3]{2,1,0:T(1,128)} %broadcast_in_dim.9), calls=%async_computation | async-start | bytes 8192 | tf_op jit(solution)/shard_map/all_to_all | solution.py:478
  11.5 0.7 %collective-permute-start.2 = (f32[4,8,2048]{2,1,0:T(8,128)S(1)}, f32[4,8,2048]{2,1,0:T(8,128)S(1)}, u32[]{:S(2)}, u32[]{:S(2)}) collective-permute-start(f32[4,8,2048]{2,1,0:T(8,128)S(1)} %pad_maximum_fusion), channel_id=1, source_target_pairs={{1,2},{3,4},{5,6},{7,8},{9,10},{11,12},{13,14},{2,1},{4,3},{6,5},{... | collective-permute-start | bytes 786440 | tf_op jit(solution)/shard_map/ppermute | solution.py:483
  12.2 0.0 copy-done
  12.2 0.0 copy-done.1
  12.2 0.0 copy-start.2
  12.2 1.2 %coast_fold.1 = (f32[3,2,32,8,128]{4,3,2,1,0:T(8,128)S(1)}, f32[8,128]{1,0:T(8,128)S(1)}) custom-call(s32[1,3]{1,0:T(1,128)S(1)} %copy-done.4, f32[256,256]{1,0:T(8,128)S(1)} %bitcast.8, f32[2,256,256]{2,1,0:T(8,128)S(1)} %bitcast.6), custom_call_target="tpu_custom_call" | custom-call | flops 45875200 | bytes 1572864 | tf_op jit(solution)/shard_map/coast_fold/pallas_call | solution.py:219
  13.4 0.0 collective-permute-done.pair.pair_state
  13.4 2.1 %all-to-all-done.links = s32[8,1,3]{2,1,0:T(1,128)S(1)} async-done(((s32[8,1,3]{2,1,0:T(1,128)}), s32[8,1,3]{2,1,0:T(1,128)S(1)}, u32[]{:S(2)}, u32[]{:S(2)}) %all-to-all-start) | async-done | bytes 128 | tf_op jit(solution)/shard_map/all_to_all | solution.py:478
  15.5 0.0 copy-done.2
  15.5 1.5 %strips.1 = f32[8,8,128]{2,1,0:T(8,128)} custom-call(s32[8,1,3]{2,1,0:T(1,128)S(1)} %all-to-all-done.links, f32[3,16,2048]{2,1,0:T(8,128)S(1)} %copy-done.2, f32[3,16,2048]{2,1,0:T(8,128)S(1)} %collective-permute-done.pair.pair_state), custom_call_target="tpu_custom_call" | custom-call | flops 20000000000 | bytes 98304 | tf_op jit(solution)/shard_map/strips/pallas_call | solution.py:449
  17.1 4.8 %all-to-all-start.1 = ((f32[8,8,128]{2,1,0:T(8,128)}), f32[8,8,128]{2,1,0:T(8,128)S(1)}, u32[]{:S(2)}, u32[]{:S(2)}) async-start(f32[8,8,128]{2,1,0:T(8,128)} %strips.1), calls=%async_computation.1 | async-start | bytes 65536 | tf_op jit(solution)/shard_map/all_to_all | solution.py:490
  21.8 0.0 collective-permute-done.1.pair_depth
  21.8 0.0 collective-permute-done.2.edge
  21.8 3.1 %basin_steps.1 = f32[3,16,2048]{2,1,0:T(8,128)} custom-call(f32[3,16,2048]{2,1,0:T(8,128)S(1)} %copy-done.2, f32[16,2048]{1,0:T(8,128)S(1)} %copy-done.3, f32[3,16,2048]{2,1,0:T(8,128)S(1)} %collective-permute-done.pair.pair_state, f32[16,2048]{1,0:T(8,128)S(1)} %collective-permute-done.1.pair_depth, f32[4,8,2048]{2,1,0:T(8,128)S(1)} %collective-permute-done.2.edge), custom_call_target="tpu_custom_call" | custom-call | flops 8388608 | bytes 1441792 | tf_op jit(solution)/shard_map/basin_steps/pallas_call | solution.py:398
  24.9 1.1 %all-to-all-done.1.ghosts = f32[8,8,128]{2,1,0:T(8,128)S(1)} async-done(((f32[8,8,128]{2,1,0:T(8,128)}), f32[8,8,128]{2,1,0:T(8,128)S(1)}, u32[]{:S(2)}, u32[]{:S(2)}) %all-to-all-start.1) | async-done | bytes 32800 | tf_op jit(solution)/shard_map/all_to_all | solution.py:490
  26.0 7.9 %coast_steps.1 = f32[3,256,256]{2,1,0:T(8,128)} custom-call(f32[8,128]{1,0:T(8,128)S(1)} %get-tuple-element.23.wet, f32[8,8,128]{2,1,0:T(8,128)S(1)} %all-to-all-done.1.ghosts, f32[3,2,32,8,128]{4,3,2,1,0:T(8,128)S(1)} %get-tuple-element.25.folded, f32[256,256]{1,0:T(8,128)S(1)} %bitcast.9, f32[2,256,256]{2,1,0:T(8,128)S(1)} %bitcast.7), custom_call_target="tpu_custom_call" | custom-call | flops 45875200 | bytes 1572864 | tf_op jit(solution)/shard_map/coast_steps/pallas_call | solution.py:303
  (2 shorter events, 0.0 us)
Async XLA Ops:
  0.6 21.2 %collective-permute-start.1 = (f32[16,2048]{1,0:T(8,128)}, f32[16,2048]{1,0:T(8,128)S(1)}, u32[]{:S(2)}, u32[]{:S(2)}) collective-permute-start(f32[16,2048]{1,0:T(8,128)} %depth), channel_id=1, source_target_pairs={{0,1},{1,0},{2,3},{3,2},{4,5},{5,4},{6,7},{7,6},{8,9},{9,8},{10,11... | collective-permute-start | bytes 393224 | tf_op jit(solution)/shard_map/ppermute | solution.py:481
  1.1 12.2 %collective-permute-start = (f32[3,16,2048]{2,1,0:T(8,128)}, f32[3,16,2048]{2,1,0:T(8,128)S(1)}, u32[]{:S(2)}, u32[]{:S(2)}) collective-permute-start(f32[3,16,2048]{2,1,0:T(8,128)} %state.1), channel_id=1, source_target_pairs={{0,1},{1,0},{2,3},{3,2},{4,5},{5,4},{6,7},{7,6},{8,9},{9,8},{10,11... | collective-permute-start | bytes 1179656 | tf_op jit(solution)/shard_map/ppermute | solution.py:481
  1.2 0.7 %copy-start.4 = (s32[1,3]{1,0:T(1,128)S(1)}, s32[1,3]{1,0:T(1,128)}, u32[]{:S(2)}) copy-start(s32[1,3]{1,0:T(1,128)} %link.1) | copy-start | bytes 40
  1.9 1.6 %copy-start.3 = (f32[16,2048]{1,0:T(8,128)S(1)}, f32[16,2048]{1,0:T(8,128)}, u32[]{:S(2)}) copy-start(f32[16,2048]{1,0:T(8,128)} %depth) | copy-start | bytes 393220
  2.5 9.7 %copy-start = (f32[1,2,256,256]{3,2,1,0:T(8,128)S(1)}, f32[1,2,256,256]{3,2,1,0:T(8,128)}, u32[]{:S(2)}) copy-start(f32[1,2,256,256]{3,2,1,0:T(8,128)} %param.8) | copy-start | bytes 1572868
  3.5 8.7 %copy-start.1 = (f32[1,256,256]{2,1,0:T(8,128)S(1)}, f32[1,256,256]{2,1,0:T(8,128)}, u32[]{:S(2)}) copy-start(f32[1,256,256]{2,1,0:T(8,128)} %param.7) | copy-start | bytes 786436
  3.6 12.0 %all-to-all-start = ((s32[8,1,3]{2,1,0:T(1,128)}), s32[8,1,3]{2,1,0:T(1,128)S(1)}, u32[]{:S(2)}, u32[]{:S(2)}) async-start(s32[8,1,3]{2,1,0:T(1,128)} %broadcast_in_dim.9), calls=%async_computation | async-start | bytes 8192 | tf_op jit(solution)/shard_map/all_to_all | solution.py:478
  11.5 10.3 %collective-permute-start.2 = (f32[4,8,2048]{2,1,0:T(8,128)S(1)}, f32[4,8,2048]{2,1,0:T(8,128)S(1)}, u32[]{:S(2)}, u32[]{:S(2)}) collective-permute-start(f32[4,8,2048]{2,1,0:T(8,128)S(1)} %pad_maximum_fusion), channel_id=1, source_target_pairs={{1,2},{3,4},{5,6},{7,8},{9,10},{11,12},{13,14},{2,1},{4,3},{6,5},{... | collective-permute-start | bytes 786440 | tf_op jit(solution)/shard_map/ppermute | solution.py:483
  12.2 3.3 %copy-start.2 = (f32[3,16,2048]{2,1,0:T(8,128)S(1)}, f32[3,16,2048]{2,1,0:T(8,128)}, u32[]{:S(2)}) copy-start(f32[3,16,2048]{2,1,0:T(8,128)} %state.1) | copy-start | bytes 1179652
  17.1 9.0 %all-to-all-start.1 = ((f32[8,8,128]{2,1,0:T(8,128)}), f32[8,8,128]{2,1,0:T(8,128)S(1)}, u32[]{:S(2)}, u32[]{:S(2)}) async-start(f32[8,8,128]{2,1,0:T(8,128)} %strips.1), calls=%async_computation.1 | async-start | bytes 65536 | tf_op jit(solution)/shard_map/all_to_all | solution.py:490
where the time goes:
time: 34.2 us; the launch traced here: 33.9 us
  starting transfers between devices  14 us (41%)
  Pallas kernels  13.7 us (40%)
  waiting for transfers between devices  3.22 us (9%)
  local copies, waits for them, and re-layouts  2.28 us (7%)
  between operations  0.71 us (2%)
    all_to_all x1, starting transfers between devices, local(): lax.all_to_all(sent, 'row', 0, 0, axis_index_groups=parity, tiled=True)  7.97 us
    pallas_call x1, Pallas kernels, coast_run(): pl.pallas_call(coast_kernel, out_shape=jax.ShapeDtypeStruct((3, cells, ce...  7.86 us
    all_to_all x1, starting transfers between devices, local(): lax.all_to_all(ghosts, 'row', 0, 0, axis_index_groups=parity, tiled=True)  4.76 us
    pallas_call x1, Pallas kernels, basin_run(): pl.pallas_call(basin_kernel, out_shape=jax.ShapeDtypeStruct((3, rows, wid...  3.11 us
    all_to_all x1, waiting for transfers between devices, local(): lax.all_to_all(sent, 'row', 0, 0, axis_index_groups=parity, tiled=True)  2.14 us
    pallas_call x1, Pallas kernels, make_strips(): pl.pallas_call(strips_kernel, out_shape=jax.ShapeDtypeStruct(tiles, jnp.f...  1.53 us
    pallas_call x1, Pallas kernels, coast_fold(): pl.pallas_call(fold_kernel, out_shape=(jax.ShapeDtypeStruct((3, 2, cells...  1.17 us
    all_to_all x1, waiting for transfers between devices, local(): lax.all_to_all(ghosts, 'row', 0, 0, axis_index_groups=parity, tiled=True)  1.08 us
  transfers between devices with their start and end apart: 5, of which 2 were waited for; matrix products, arithmetic and copies ran while one was open for 5% of the time, Pallas kernels for 17%

commit v1 on v0

--- a/solution.py
+++ b/solution.py
@@ -465,16 +465,14 @@
     chips.insert(0, chips.pop(len(chips) - 1 - devices // 4))
     parity = [[2 * chip + p for chip in chips] for p in range(2)]
     sent = jnp.broadcast_to(coast_link, (devices // 2,) + coast_link.shape)
-    sent, later_state = lax.optimization_barrier((sent, basin_state))
     start = odd * (basin_depth.shape[0] - HALO)
     edge = jnp.concatenate(
         [
-            lax.dynamic_slice_in_dim(later_state, start, HALO, axis=1),
+            lax.dynamic_slice_in_dim(basin_state, start, HALO, axis=1),
             lax.dynamic_slice_in_dim(basin_depth, start, HALO, axis=0)[None],
         ],
         axis=0,
     )
-    sent, edge = lax.optimization_barrier((sent, edge))
     links = lax.all_to_all(sent, "row", 0, 0, axis_index_groups=parity, tiled=True)
 
     twins = [(i, i ^ 1) for i in range(devices)]

time: 34.2 us -> 34.3 us (level)
  waiting for transfers between devices: 3.22 us -> 1.38 us
  starting transfers between devices: 14 us -> 15.8 us
    all_to_all x1, starting transfers between devices: 4.76 us -> 6.67 us  [local(): lax.all_to_all(ghosts, 'row', 0, 0, axis_index_groups=parity, tiled=True)]
    all_to_all x1, waiting for transfers between devices: 2.14 us -> 0.3 us  [local(): lax.all_to_all(sent, 'row', 0, 0, axis_index_groups=parity, tiled=True)]
  transfers between devices with their start and end apart: 5 -> 5, of which waited for: 2 -> 2; matrix products, arithmetic and copies ran while one was open for 5% -> 3% of each run, Pallas kernels for 17% -> 17%
where the time goes in v1:
time: 34.3 us; the launch traced here: 34 us
  starting transfers between devices  15.8 us (46%)
  Pallas kernels  13.7 us (40%)
  local copies, waits for them, and re-layouts  2.4 us (7%)
  waiting for transfers between devices  1.38 us (4%)
  between operations  0.7 us (2%)
    pallas_call x1, Pallas kernels, coast_run(): pl.pallas_call(coast_kernel, out_shape=jax.ShapeDtypeStruct((3, cells, ce...  7.86 us
    all_to_all x1, starting transfers between devices, local(): lax.all_to_all(sent, 'row', 0, 0, axis_index_groups=parity, tiled=True)  7.84 us
    all_to_all x1, starting transfers between devices, local(): lax.all_to_all(ghosts, 'row', 0, 0, axis_index_groups=parity, tiled=True)  6.67 us
    pallas_call x1, Pallas kernels, basin_run(): pl.pallas_call(basin_kernel, out_shape=jax.ShapeDtypeStruct((3, rows, wid...  3.11 us
    pallas_call x1, Pallas kernels, make_strips(): pl.pallas_call(strips_kernel, out_shape=jax.ShapeDtypeStruct(tiles, jnp.f...  1.53 us
    pallas_call x1, Pallas kernels, coast_fold(): pl.pallas_call(fold_kernel, out_shape=(jax.ShapeDtypeStruct((3, 2, cells...  1.16 us
    all_to_all x1, waiting for transfers between devices, local(): lax.all_to_all(ghosts, 'row', 0, 0, axis_index_groups=parity, tiled=True)  1.08 us
    dynamic_slice x1, local copies, waits for them, and re-layouts, local(): lax.dynamic_slice_in_dim(basin_state, start, HALO, axis=1)  1.01 us
  transfers between devices with their start and end apart: 5, of which 2 were waited for; matrix products, arithmetic and copies ran while one was open for 3% of the time, Pallas kernels for 17%

profile of v1, /device:TPU:0, one launch (start us, length us, event | category | flops | bytes accessed | tf_op | source)
XLA Modules:
  0.0 34.0 jit_solution(5336847511700503861)
XLA Ops:
  0.6 0.0 copy-start.4
  0.6 0.6 %copy-done.4 = s32[1,3]{1,0:T(1,128)S(1)} copy-done((s32[1,3]{1,0:T(1,128)S(1)}, s32[1,3]{1,0:T(1,128)}, u32[]{:S(2)}) %copy-start.4) | copy-done | bytes 36
  1.3 0.6 %broadcast_in_dim.9 = s32[8,1,3]{2,1,0:T(1,128)} broadcast(s32[3]{0:T(128)S(1)} %bitcast.10), dimensions={2} | broadcast | bytes 108 | tf_op jit(solution)/shard_map/broadcast_in_dim | solution.py:467
  1.9 7.8 %all-to-all-start = ((s32[8,1,3]{2,1,0:T(1,128)}), s32[8,1,3]{2,1,0:T(1,128)S(1)}, u32[]{:S(2)}, u32[]{:S(2)}) async-start(s32[8,1,3]{2,1,0:T(1,128)} %broadcast_in_dim.9), calls=%async_computation | async-start | bytes 8192 | tf_op jit(solution)/shard_map/all_to_all | solution.py:476
  9.7 0.0 collective-permute-start.1
  9.7 0.5 %collective-permute-start = (f32[3,16,2048]{2,1,0:T(8,128)}, f32[3,16,2048]{2,1,0:T(8,128)S(1)}, u32[]{:S(2)}, u32[]{:S(2)}) collective-permute-start(f32[3,16,2048]{2,1,0:T(8,128)} %state.1), channel_id=1, source_target_pairs={{0,1},{1,0},{2,3},{3,2},{4,5},{5,4},{6,7},{7,6},{8,9},{9,8},{10,11... | collective-permute-start | bytes 1179656 | tf_op jit(solution)/shard_map/ppermute | solution.py:479
  10.2 0.0 copy-start.3
  10.2 0.0 copy-start
  10.2 1.0 %constant_dynamic-slice_fusion = f32[3,8,2048]{2,1,0:T(8,128)S(1)} fusion(f32[3,16,2048]{2,1,0:T(8,128)} %state.1, s32[]{:T(128)S(6)} %select_n.12), kind=kLoop, calls=%fused_computation.2 | loop fusion | bytes 393220 | tf_op jit(solution)/shard_map/dynamic_slice | solution.py:471
  11.2 0.0 copy-done.3
  11.3 0.0 copy-start.1
  11.3 0.8 %collective-permute-start.2 = (f32[4,8,2048]{2,1,0:T(8,128)S(1)}, f32[4,8,2048]{2,1,0:T(8,128)S(1)}, u32[]{:S(2)}, u32[]{:S(2)}) collective-permute-start(f32[4,8,2048]{2,1,0:T(8,128)S(1)} %pad_maximum_fusion), channel_id=1, source_target_pairs={{1,2},{3,4},{5,6},{7,8},{9,10},{11,12},{13,14},{2,1},{4,3},{6,5},{... | collective-permute-start | bytes 786440 | tf_op jit(solution)/shard_map/ppermute | solution.py:481
  12.1 0.0 copy-done
  12.1 0.1 copy-done.1
  12.3 0.0 copy-start.2
  12.3 1.2 %coast_fold.1 = (f32[3,2,32,8,128]{4,3,2,1,0:T(8,128)S(1)}, f32[8,128]{1,0:T(8,128)S(1)}) custom-call(s32[1,3]{1,0:T(1,128)S(1)} %copy-done.4, f32[256,256]{1,0:T(8,128)S(1)} %bitcast.8, f32[2,256,256]{2,1,0:T(8,128)S(1)} %bitcast.6), custom_call_target="tpu_custom_call" | custom-call | flops 45875200 | bytes 1572864 | tf_op jit(solution)/shard_map/coast_fold/pallas_call | solution.py:219
  13.4 0.0 collective-permute-done.pair.pair_state
  13.4 0.3 all-to-all-done.links
  13.7 0.0 copy-done.2
  13.7 1.5 %strips.1 = f32[8,8,128]{2,1,0:T(8,128)} custom-call(s32[8,1,3]{2,1,0:T(1,128)S(1)} %all-to-all-done.links, f32[3,16,2048]{2,1,0:T(8,128)S(1)} %copy-done.2, f32[3,16,2048]{2,1,0:T(8,128)S(1)} %collective-permute-done.pair.pair_state), custom_call_target="tpu_custom_call" | custom-call | flops 20000000000 | bytes 98304 | tf_op jit(solution)/shard_map/strips/pallas_call | solution.py:449
  15.3 6.7 %all-to-all-start.1 = ((f32[8,8,128]{2,1,0:T(8,128)}), f32[8,8,128]{2,1,0:T(8,128)S(1)}, u32[]{:S(2)}, u32[]{:S(2)}) async-start(f32[8,8,128]{2,1,0:T(8,128)} %strips.1), calls=%async_computation.1 | async-start | bytes 65536 | tf_op jit(solution)/shard_map/all_to_all | solution.py:488
  21.9 0.0 collective-permute-done.1.pair_depth
  21.9 0.0 collective-permute-done.2.edge
  21.9 3.1 %basin_steps.1 = f32[3,16,2048]{2,1,0:T(8,128)} custom-call(f32[3,16,2048]{2,1,0:T(8,128)S(1)} %copy-done.2, f32[16,2048]{1,0:T(8,128)S(1)} %copy-done.3, f32[3,16,2048]{2,1,0:T(8,128)S(1)} %collective-permute-done.pair.pair_state, f32[16,2048]{1,0:T(8,128)S(1)} %collective-permute-done.1.pair_depth, f32[4,8,2048]{2,1,0:T(8,128)S(1)} %collective-permute-done.2.edge), custom_call_target="tpu_custom_call" | custom-call | flops 8388608 | bytes 1441792 | tf_op jit(solution)/shard_map/basin_steps/pallas_call | solution.py:398
  25.1 1.1 %all-to-all-done.1.ghosts = f32[8,8,128]{2,1,0:T(8,128)S(1)} async-done(((f32[8,8,128]{2,1,0:T(8,128)}), f32[8,8,128]{2,1,0:T(8,128)S(1)}, u32[]{:S(2)}, u32[]{:S(2)}) %all-to-all-start.1) | async-done | bytes 32800 | tf_op jit(solution)/shard_map/all_to_all | solution.py:488
  26.1 7.9 %coast_steps.1 = f32[3,256,256]{2,1,0:T(8,128)} custom-call(f32[8,128]{1,0:T(8,128)S(1)} %get-tuple-element.15.wet, f32[8,8,128]{2,1,0:T(8,128)S(1)} %all-to-all-done.1.ghosts, f32[3,2,32,8,128]{4,3,2,1,0:T(8,128)S(1)} %get-tuple-element.17.folded, f32[256,256]{1,0:T(8,128)S(1)} %bitcast.9, f32[2,256,256]{2,1,0:T(8,128)S(1)} %bitcast.7), custom_call_target="tpu_custom_call" | custom-call | flops 45875200 | bytes 1572864 | tf_op jit(solution)/shard_map/coast_steps/pallas_call | solution.py:303
  (2 shorter events, 0.0 us)
Async XLA Ops:
  0.6 0.7 %copy-start.4 = (s32[1,3]{1,0:T(1,128)S(1)}, s32[1,3]{1,0:T(1,128)}, u32[]{:S(2)}) copy-start(s32[1,3]{1,0:T(1,128)} %link.1) | copy-start | bytes 40
  1.9 11.9 %all-to-all-start = ((s32[8,1,3]{2,1,0:T(1,128)}), s32[8,1,3]{2,1,0:T(1,128)S(1)}, u32[]{:S(2)}, u32[]{:S(2)}) async-start(s32[8,1,3]{2,1,0:T(1,128)} %broadcast_in_dim.9), calls=%async_computation | async-start | bytes 8192 | tf_op jit(solution)/shard_map/all_to_all | solution.py:476
  9.7 12.2 %collective-permute-start.1 = (f32[16,2048]{1,0:T(8,128)}, f32[16,2048]{1,0:T(8,128)S(1)}, u32[]{:S(2)}, u32[]{:S(2)}) collective-permute-start(f32[16,2048]{1,0:T(8,128)} %depth), channel_id=1, source_target_pairs={{0,1},{1,0},{2,3},{3,2},{4,5},{5,4},{6,7},{7,6},{8,9},{9,8},{10,11... | collective-permute-start | bytes 393224 | tf_op jit(solution)/shard_map/ppermute | solution.py:479
  9.7 3.7 %collective-permute-start = (f32[3,16,2048]{2,1,0:T(8,128)}, f32[3,16,2048]{2,1,0:T(8,128)S(1)}, u32[]{:S(2)}, u32[]{:S(2)}) collective-permute-start(f32[3,16,2048]{2,1,0:T(8,128)} %state.1), channel_id=1, source_target_pairs={{0,1},{1,0},{2,3},{3,2},{4,5},{5,4},{6,7},{7,6},{8,9},{9,8},{10,11... | collective-permute-start | bytes 1179656 | tf_op jit(solution)/shard_map/ppermute | solution.py:479
  10.2 1.0 %copy-start.3 = (f32[16,2048]{1,0:T(8,128)S(1)}, f32[16,2048]{1,0:T(8,128)}, u32[]{:S(2)}) copy-start(f32[16,2048]{1,0:T(8,128)} %depth) | copy-start | bytes 393220
  10.2 1.9 %copy-start = (f32[1,2,256,256]{3,2,1,0:T(8,128)S(1)}, f32[1,2,256,256]{3,2,1,0:T(8,128)}, u32[]{:S(2)}) copy-start(f32[1,2,256,256]{3,2,1,0:T(8,128)} %param.8) | copy-start | bytes 1572868
  11.3 1.0 %copy-start.1 = (f32[1,256,256]{2,1,0:T(8,128)S(1)}, f32[1,256,256]{2,1,0:T(8,128)}, u32[]{:S(2)}) copy-start(f32[1,256,256]{2,1,0:T(8,128)} %param.7) | copy-start | bytes 786436
  11.3 10.6 %collective-permute-start.2 = (f32[4,8,2048]{2,1,0:T(8,128)S(1)}, f32[4,8,2048]{2,1,0:T(8,128)S(1)}, u32[]{:S(2)}, u32[]{:S(2)}) collective-permute-start(f32[4,8,2048]{2,1,0:T(8,128)S(1)} %pad_maximum_fusion), channel_id=1, source_target_pairs={{1,2},{3,4},{5,6},{7,8},{9,10},{11,12},{13,14},{2,1},{4,3},{6,5},{... | collective-permute-start | bytes 786440 | tf_op jit(solution)/shard_map/ppermute | solution.py:481
  12.3 1.5 %copy-start.2 = (f32[3,16,2048]{2,1,0:T(8,128)S(1)}, f32[3,16,2048]{2,1,0:T(8,128)}, u32[]{:S(2)}) copy-start(f32[3,16,2048]{2,1,0:T(8,128)} %state.1) | copy-start | bytes 1179652
  15.3 10.9 %all-to-all-start.1 = ((f32[8,8,128]{2,1,0:T(8,128)}), f32[8,8,128]{2,1,0:T(8,128)S(1)}, u32[]{:S(2)}, u32[]{:S(2)}) async-start(f32[8,8,128]{2,1,0:T(8,128)} %strips.1), calls=%async_computation.1 | async-start | bytes 65536 | tf_op jit(solution)/shard_map/all_to_all | solution.py:488

commit v2 on v1

--- a/solution.py
+++ b/solution.py
@@ -480,12 +480,11 @@
     across = [(i, i + 1) for i in range(1, devices - 1, 2)]
     edge = lax.ppermute(edge, "row", across + [(j, i) for i, j in across])
 
+    ghosts = make_strips(links, basin_state, pair_state)
+    basin_depth, coast_depth, ghosts = lax.optimization_barrier((basin_depth, coast_depth, ghosts))
+    ghosts = lax.all_to_all(ghosts, "row", 0, 0, axis_index_groups=parity, tiled=True)
     depth, flow = coast_depth[0], coast_flow[0]
     folded, wet = coast_fold(coast_link, depth, flow)
-    pair_state, folded = lax.optimization_barrier((pair_state, folded))
-    ghosts = make_strips(links, basin_state, pair_state)
-    basin_depth, ghosts = lax.optimization_barrier((basin_depth, ghosts))
-    ghosts = lax.all_to_all(ghosts, "row", 0, 0, axis_index_groups=parity, tiled=True)
     basin_out = basin_run(basin_state, basin_depth, pair_state, pair_depth, edge)
     folded, basin_out = lax.optimization_barrier((folded, basin_out))
     coast_out = coast_run(wet, ghosts, folded, depth, flow)

time: 34.3 us -> 33.2 us (0.968)
  starting transfers between devices: 15.8 us -> 14.6 us
    all_to_all x1, waiting for transfers between devices: 0.3 us -> 1.63 us  [local(): lax.all_to_all(sent, 'row', 0, 0, axis_index_groups=parity, tiled=True)]
    all_to_all x1, starting transfers between devices: 6.67 us -> 5.44 us  [local(): lax.all_to_all(ghosts, 'row', 0, 0, axis_index_groups=parity, tiled=True)]
    all_to_all x1, waiting for transfers between devices: 1.08 us -> 0.01 us  [local(): lax.all_to_all(ghosts, 'row', 0, 0, axis_index_groups=parity, tiled=True)]
  transfers between devices with their start and end apart: 5 -> 5, of which waited for: 2 -> 1; matrix products, arithmetic and copies ran while one was open for 3% -> 3% of each run, Pallas kernels for 17% -> 18%
where the time goes in v2:
time: 33.2 us; the launch traced here: 32.9 us
  starting transfers between devices  14.6 us (44%)
  Pallas kernels  13.7 us (41%)
  local copies, waits for them, and re-layouts  2.26 us (7%)
  waiting for transfers between devices  1.64 us (5%)
  between operations  0.69 us (2%)
    pallas_call x1, Pallas kernels, coast_run(): pl.pallas_call(coast_kernel, out_shape=jax.ShapeDtypeStruct((3, cells, ce...  7.87 us
    all_to_all x1, starting transfers between devices, local(): lax.all_to_all(sent, 'row', 0, 0, axis_index_groups=parity, tiled=True)  7.84 us
    all_to_all x1, starting transfers between devices, local(): lax.all_to_all(ghosts, 'row', 0, 0, axis_index_groups=parity, tiled=True)  5.44 us
    pallas_call x1, Pallas kernels, basin_run(): pl.pallas_call(basin_kernel, out_shape=jax.ShapeDtypeStruct((3, rows, wid...  3.11 us
    all_to_all x1, waiting for transfers between devices, local(): lax.all_to_all(sent, 'row', 0, 0, axis_index_groups=parity, tiled=True)  1.63 us
    pallas_call x1, Pallas kernels, make_strips(): pl.pallas_call(strips_kernel, out_shape=jax.ShapeDtypeStruct(tiles, jnp.f...  1.53 us
    pallas_call x1, Pallas kernels, coast_fold(): pl.pallas_call(fold_kernel, out_shape=(jax.ShapeDtypeStruct((3, 2, cells...  1.17 us
    dynamic_slice x1, local copies, waits for them, and re-layouts, local(): lax.dynamic_slice_in_dim(basin_state, start, HALO, axis=1)  0.98 us
  transfers between devices with their start and end apart: 5, of which 1 were waited for; matrix products, arithmetic and copies ran while one was open for 3% of the time, Pallas kernels for 18%

profile of v2, /device:TPU:0, one launch (start us, length us, event | category | flops | bytes accessed | tf_op | source)
XLA Modules:
  0.0 32.9 jit_solution(6365339972864458219)
XLA Ops:
  0.6 0.0 copy-start.4
  0.6 0.6 %copy-done.4 = s32[1,3]{1,0:T(1,128)S(1)} copy-done((s32[1,3]{1,0:T(1,128)S(1)}, s32[1,3]{1,0:T(1,128)}, u32[]{:S(2)}) %copy-start.4) | copy-done | bytes 36
  1.3 0.6 %broadcast_in_dim.9 = s32[8,1,3]{2,1,0:T(1,128)} broadcast(s32[3]{0:T(128)S(1)} %bitcast.10), dimensions={2} | broadcast | bytes 108 | tf_op jit(solution)/shard_map/broadcast_in_dim | solution.py:467
  1.9 7.8 %all-to-all-start = ((s32[8,1,3]{2,1,0:T(1,128)}), s32[8,1,3]{2,1,0:T(1,128)S(1)}, u32[]{:S(2)}, u32[]{:S(2)}) async-start(s32[8,1,3]{2,1,0:T(1,128)} %broadcast_in_dim.9), calls=%async_computation | async-start | bytes 8192 | tf_op jit(solution)/shard_map/all_to_all | solution.py:476
  9.7 0.0 collective-permute-start.1
  9.7 0.5 %collective-permute-start = (f32[3,16,2048]{2,1,0:T(8,128)}, f32[3,16,2048]{2,1,0:T(8,128)S(1)}, u32[]{:S(2)}, u32[]{:S(2)}) collective-permute-start(f32[3,16,2048]{2,1,0:T(8,128)} %state.1), channel_id=1, source_target_pairs={{0,1},{1,0},{2,3},{3,2},{4,5},{5,4},{6,7},{7,6},{8,9},{9,8},{10,11... | collective-permute-start | bytes 1179656 | tf_op jit(solution)/shard_map/ppermute | solution.py:479
  10.2 0.0 copy-start.3
  10.2 1.0 %constant_dynamic-slice_fusion = f32[3,8,2048]{2,1,0:T(8,128)S(1)} fusion(f32[3,16,2048]{2,1,0:T(8,128)} %state.1, s32[]{:T(128)S(6)} %select_n.12), kind=kLoop, calls=%fused_computation.2 | loop fusion | bytes 393220 | tf_op jit(solution)/shard_map/dynamic_slice | solution.py:471
  11.2 0.0 copy-done.3
  11.2 0.0 copy-start.2
  11.3 0.8 %collective-permute-start.2 = (f32[4,8,2048]{2,1,0:T(8,128)S(1)}, f32[4,8,2048]{2,1,0:T(8,128)S(1)}, u32[]{:S(2)}, u32[]{:S(2)}) collective-permute-start(f32[4,8,2048]{2,1,0:T(8,128)S(1)} %pad_maximum_fusion), channel_id=1, source_target_pairs={{1,2},{3,4},{5,6},{7,8},{9,10},{11,12},{13,14},{2,1},{4,3},{6,5},{... | collective-permute-start | bytes 786440 | tf_op jit(solution)/shard_map/ppermute | solution.py:481
  12.1 1.6 %all-to-all-done.links = s32[8,1,3]{2,1,0:T(1,128)S(1)} async-done(((s32[8,1,3]{2,1,0:T(1,128)}), s32[8,1,3]{2,1,0:T(1,128)S(1)}, u32[]{:S(2)}, u32[]{:S(2)}) %all-to-all-start) | async-done | bytes 128 | tf_op jit(solution)/shard_map/all_to_all | solution.py:476
  13.7 0.0 collective-permute-done.pair.pair_state
  13.7 0.0 copy-done.2
  13.7 1.5 %strips.1 = f32[8,8,128]{2,1,0:T(8,128)} custom-call(s32[8,1,3]{2,1,0:T(1,128)S(1)} %all-to-all-done.links, f32[3,16,2048]{2,1,0:T(8,128)S(1)} %copy-done.2, f32[3,16,2048]{2,1,0:T(8,128)S(1)} %collective-permute-done.pair.pair_state), custom_call_target="tpu_custom_call" | custom-call | flops 20000000000 | bytes 98304 | tf_op jit(solution)/shard_map/strips/pallas_call | solution.py:449
  15.3 5.4 %all-to-all-start.1 = ((f32[8,8,128]{2,1,0:T(8,128)}), f32[8,8,128]{2,1,0:T(8,128)S(1)}, u32[]{:S(2)}, u32[]{:S(2)}) async-start(f32[8,8,128]{2,1,0:T(8,128)} %strips.1), calls=%async_computation.1 | async-start | bytes 65536 | tf_op jit(solution)/shard_map/all_to_all | solution.py:485
  20.7 0.0 copy-start
  20.7 0.0 copy-start.1
  20.7 0.0 collective-permute-done.1.pair_depth
  20.7 0.0 collective-permute-done.2.edge
  20.7 3.1 %basin_steps.1 = f32[3,16,2048]{2,1,0:T(8,128)} custom-call(f32[3,16,2048]{2,1,0:T(8,128)S(1)} %copy-done.2, f32[16,2048]{1,0:T(8,128)S(1)} %copy-done.3, f32[3,16,2048]{2,1,0:T(8,128)S(1)} %collective-permute-done.pair.pair_state, f32[16,2048]{1,0:T(8,128)S(1)} %collective-permute-done.1.pair_depth, f32[4,8,2048]{2,1,0:T(8,128)S(1)} %collective-permute-done.2.edge), custom_call_target="tpu_custom_call" | custom-call | flops 8388608 | bytes 1441792 | tf_op jit(solution)/shard_map/basin_steps/pallas_call | solution.py:398
  23.8 0.0 copy-done
  23.9 0.0 copy-done.1
  23.9 1.2 %coast_fold.1 = (f32[3,2,32,8,128]{4,3,2,1,0:T(8,128)S(1)}, f32[8,128]{1,0:T(8,128)S(1)}) custom-call(s32[1,3]{1,0:T(1,128)S(1)} %copy-done.4, f32[256,256]{1,0:T(8,128)S(1)} %bitcast.8, f32[2,256,256]{2,1,0:T(8,128)S(1)} %bitcast.6), custom_call_target="tpu_custom_call" | custom-call | flops 45875200 | bytes 1572864 | tf_op jit(solution)/shard_map/coast_fold/pallas_call | solution.py:219
  25.0 0.0 all-to-all-done.1.ghosts
  25.0 7.9 %coast_steps.1 = f32[3,256,256]{2,1,0:T(8,128)} custom-call(f32[8,128]{1,0:T(8,128)S(1)} %get-tuple-element.13.wet, f32[8,8,128]{2,1,0:T(8,128)S(1)} %all-to-all-done.1.ghosts, f32[3,2,32,8,128]{4,3,2,1,0:T(8,128)S(1)} %get-tuple-element.15.folded, f32[256,256]{1,0:T(8,128)S(1)} %bitcast.9, f32[2,256,256]{2,1,0:T(8,128)S(1)} %bitcast.7), custom_call_target="tpu_custom_call" | custom-call | flops 45875200 | bytes 1572864 | tf_op jit(solution)/shard_map/coast_steps/pallas_call | solution.py:303
  (2 shorter events, 0.0 us)
Async XLA Ops:
  0.6 0.7 %copy-start.4 = (s32[1,3]{1,0:T(1,128)S(1)}, s32[1,3]{1,0:T(1,128)}, u32[]{:S(2)}) copy-start(s32[1,3]{1,0:T(1,128)} %link.1) | copy-start | bytes 40
  1.9 11.9 %all-to-all-start = ((s32[8,1,3]{2,1,0:T(1,128)}), s32[8,1,3]{2,1,0:T(1,128)S(1)}, u32[]{:S(2)}, u32[]{:S(2)}) async-start(s32[8,1,3]{2,1,0:T(1,128)} %broadcast_in_dim.9), calls=%async_computation | async-start | bytes 8192 | tf_op jit(solution)/shard_map/all_to_all | solution.py:476
  9.7 11.0 %collective-permute-start.1 = (f32[16,2048]{1,0:T(8,128)}, f32[16,2048]{1,0:T(8,128)S(1)}, u32[]{:S(2)}, u32[]{:S(2)}) collective-permute-start(f32[16,2048]{1,0:T(8,128)} %depth), channel_id=1, source_target_pairs={{0,1},{1,0},{2,3},{3,2},{4,5},{5,4},{6,7},{7,6},{8,9},{9,8},{10,11... | collective-permute-start | bytes 393224 | tf_op jit(solution)/shard_map/ppermute | solution.py:479
  9.7 4.0 %collective-permute-start = (f32[3,16,2048]{2,1,0:T(8,128)}, f32[3,16,2048]{2,1,0:T(8,128)S(1)}, u32[]{:S(2)}, u32[]{:S(2)}) collective-permute-start(f32[3,16,2048]{2,1,0:T(8,128)} %state.1), channel_id=1, source_target_pairs={{0,1},{1,0},{2,3},{3,2},{4,5},{5,4},{6,7},{7,6},{8,9},{9,8},{10,11... | collective-permute-start | bytes 1179656 | tf_op jit(solution)/shard_map/ppermute | solution.py:479
  10.2 1.0 %copy-start.3 = (f32[16,2048]{1,0:T(8,128)S(1)}, f32[16,2048]{1,0:T(8,128)}, u32[]{:S(2)}) copy-start(f32[16,2048]{1,0:T(8,128)} %depth) | copy-start | bytes 393220
  11.2 2.5 %copy-start.2 = (f32[3,16,2048]{2,1,0:T(8,128)S(1)}, f32[3,16,2048]{2,1,0:T(8,128)}, u32[]{:S(2)}) copy-start(f32[3,16,2048]{2,1,0:T(8,128)} %state.1) | copy-start | bytes 1179652
  11.3 9.4 %collective-permute-start.2 = (f32[4,8,2048]{2,1,0:T(8,128)S(1)}, f32[4,8,2048]{2,1,0:T(8,128)S(1)}, u32[]{:S(2)}, u32[]{:S(2)}) collective-permute-start(f32[4,8,2048]{2,1,0:T(8,128)S(1)} %pad_maximum_fusion), channel_id=1, source_target_pairs={{1,2},{3,4},{5,6},{7,8},{9,10},{11,12},{13,14},{2,1},{4,3},{6,5},{... | collective-permute-start | bytes 786440 | tf_op jit(solution)/shard_map/ppermute | solution.py:481
  15.3 9.7 %all-to-all-start.1 = ((f32[8,8,128]{2,1,0:T(8,128)}), f32[8,8,128]{2,1,0:T(8,128)S(1)}, u32[]{:S(2)}, u32[]{:S(2)}) async-start(f32[8,8,128]{2,1,0:T(8,128)} %strips.1), calls=%async_computation.1 | async-start | bytes 65536 | tf_op jit(solution)/shard_map/all_to_all | solution.py:485
  20.7 3.1 %copy-start = (f32[1,2,256,256]{3,2,1,0:T(8,128)S(1)}, f32[1,2,256,256]{3,2,1,0:T(8,128)}, u32[]{:S(2)}) copy-start(f32[1,2,256,256]{3,2,1,0:T(8,128)} %param.8) | copy-start | bytes 1572868
  20.7 3.1 %copy-start.1 = (f32[1,256,256]{2,1,0:T(8,128)S(1)}, f32[1,256,256]{2,1,0:T(8,128)}, u32[]{:S(2)}) copy-start(f32[1,256,256]{2,1,0:T(8,128)} %param.7) | copy-start | bytes 786436
